TPU v7x, 128 devices: a whole 4x4x4 slice. The times are simulated.
128 devices in a mesh: mesh: 32 (over y, x, core), state: 4 (over z).
Axes of the slice: x: 4, y: 4, z: 4, core: 2. Of those that a mesh axis runs over, the one named last changes fastest.
Arguments:
- kern_blocks: bfloat16 [768, 16, 128, 128], P('mesh'), may hold values from 4.296875e-06 to 0.13744531
- kern_cols: int32 [768, 16], P('mesh'), may hold values from 0 to 767, as said below
- state_kernel: bfloat16 [512, 512], replicated, may hold values from 0 to 0.61, as said below
- start_v: float32 [98304, 512], P('mesh', 'state'), may hold values from 0.5 to 5
- mu: float32 [98304, 512], P(('mesh', 'state')), may hold values from 0.2 to 2
- nu: float32 [98304, 512], P('mesh', 'state'), may hold values from 0.2 to 2
Outputs:
- potential_u: float32 [98304, 512], P(('mesh', 'state'))
- potential_v: float32 [98304, 512], P('mesh', 'state')
Inputs may be any that keep to these rules, and one draw needn't show every extreme that they name: `kern_cols`: each block row names 16 different block columns, its own block among them. The block rows held by index d of mesh (rows d * 24 to (d + 1) * 24 - 1) refer, among the blocks of index d - 1 and d + 1 (wrapping around 32), only to the last 6 blocks of d - 1 and the first 6 blocks of d + 1, and to all of them; among the blocks of every other index, to at most 2 distinct blocks, and to exactly 2 of index d + 2. How many other indices they reach differs from index to index. `state_kernel`: each row has a positive diagonal entry.
All inputs are finite; a program needn't handle non-finite values.
Results may differ from a plain program's by a relative error of at most 0.0033.
Values may be sent and summed in bfloat16 or wider, within the bound.
A program may use at most 192 MiB of HBM per device.

v0:
```python
import jax
import jax.numpy as jnp
from jax import lax
from jax.sharding import PartitionSpec as P

ITERS = 2
CAP = 6


def request_plan(owners, places, remote, peer_count, block_rows, width):
    peer_ids = jnp.arange(peer_count, dtype=jnp.int32)
    place_ids = jnp.arange(block_rows, dtype=jnp.int32)
    matches = (
        remote[:, None, None]
        & (owners[:, None, None] == peer_ids[None, :, None])
        & (places[:, None, None] == place_ids[None, None, :])
    )
    matches = matches.astype(jnp.int32)
    needed = jnp.max(matches, axis=0)
    ranking = jnp.cumsum(needed, axis=1) - needed
    ref_slots = jnp.sum(matches * ranking[None, :, :], axis=(1, 2))
    slot_ids = jnp.arange(width, dtype=jnp.int32)
    selected = needed[:, :, None] * (ranking[:, :, None] == slot_ids[None, None, :]).astype(
        jnp.int32
    )
    requests = jnp.sum(selected * place_ids[None, :, None], axis=1)
    return (ref_slots, requests)


def rounded_sum(values):
    return lax.optimization_barrier(values.astype(jnp.bfloat16)).astype(jnp.float32)


def per_device(kern_blocks, kern_cols, state_kernel, start_v, mu, nu):
    block_rows, degree, block_size, _ = kern_blocks.shape
    local_rows, state_cols = start_v.shape
    peer_count = lax.axis_size("mesh")
    state_count = lax.axis_size("state")
    my_index = lax.axis_index("mesh")
    flat_cols = kern_cols.reshape(-1)
    owners = flat_cols // block_rows
    places = flat_cols % block_rows
    remote = owners != my_index
    ref_slots, requests = request_plan(owners, places, remote, peer_count, block_rows, CAP)
    asked = lax.all_to_all(requests, "mesh", split_axis=0, concat_axis=0, tiled=True)
    sources = jnp.where(remote, block_rows + owners * CAP + ref_slots, places)
    table_size = block_rows + peer_count * CAP
    flat_asked = asked.reshape(-1)
    values = start_v
    potential_u = mu
    for sweep in range(ITERS):
        blocks = values.astype(jnp.bfloat16).reshape(block_rows, block_size, state_cols)
        incoming = lax.all_to_all(blocks[asked], "mesh", split_axis=0, concat_axis=0, tiled=True)
        table = jnp.concatenate([blocks, incoming.reshape(-1, block_size, state_cols)], axis=0)
        picked = table[sources].reshape(block_rows, degree, block_size, state_cols)
        applied = jnp.einsum(
            "rkab,rkbc->rac", kern_blocks, picked, preferred_element_type=jnp.float32
        )
        pieces = applied.astype(jnp.bfloat16).reshape(
            state_count, local_rows // state_count, state_cols
        )
        mixed = jnp.einsum(
            "xrl,jl->xrj",
            lax.all_to_all(pieces, "state", split_axis=0, concat_axis=2, tiled=True),
            state_kernel,
            preferred_element_type=jnp.float32,
        )
        potential_u = mu / mixed[0]
        back_rows = jnp.dot(
            potential_u.astype(jnp.bfloat16), state_kernel, preferred_element_type=jnp.float32
        ).astype(jnp.bfloat16)
        returned = lax.all_to_all(back_rows, "state", split_axis=1, concat_axis=0, tiled=True)
        returned = returned.reshape(block_rows, block_size, state_cols)
        spread = jnp.einsum(
            "rkab,rac->rkbc", kern_blocks, returned, preferred_element_type=jnp.float32
        )
        contrib_table = jax.ops.segment_sum(
            spread.reshape(-1, block_size, state_cols), sources, num_segments=table_size
        )
        own_part = rounded_sum(contrib_table[:block_rows])
        outgoing = (
            contrib_table[block_rows:]
            .reshape(peer_count, CAP, block_size, state_cols)
            .astype(jnp.bfloat16)
        )
        arriving = lax.all_to_all(outgoing, "mesh", split_axis=0, concat_axis=0, tiled=True)
        arriving = arriving.reshape(-1, block_size, state_cols).astype(jnp.float32)
        totals = own_part + jax.ops.segment_sum(arriving, flat_asked, num_segments=block_rows)
        values = nu / totals.reshape(local_rows, state_cols)
    return (potential_u, values)


def solution(mesh):
    placed = (
        P("mesh", None, None, None),
        P("mesh", None),
        P(),
        P("mesh", "state"),
        P(("mesh", "state"), None),
        P("mesh", "state"),
    )
    return jax.shard_map(
        per_device,
        mesh=mesh,
        in_specs=placed,
        out_specs=(P(("mesh", "state"), None), P("mesh", "state")),
        check_vma=False,
    )
```

profile of v0, /device:TPU:0, one launch (start us, length us, event | category | flops | bytes accessed | tf_op | source)
XLA Modules:
  0.0 854.1 jit_solution(14254302515081292741)
XLA Ops:
  0.6 0.8 broadcast_divide_fusion
  1.4 0.7 sign_compare_fusion
  2.2 0.1 rem.49
  2.4 0.1 copy.36
  2.5 0.1 ne.120
  2.7 0.6 fusion.1
  3.4 0.2 reduce_window_sum.11
  3.7 0.7 copy.44
  4.4 7.4 all-to-all-start
  11.8 1.5 convert_element_type.63
  13.3 5.8 all-to-all-done
  19.1 0.1 reshape.347
  19.2 7.9 gather_fusion
  27.1 5.4 all-to-all-start.1
  32.7 0.1 ne.115
  32.8 0.2 fusion.2
  33.1 77.2 %all-to-all-done.1 = bf16[32,6,128,128]{3,2,1,0:T(8,128)(2,1)} async-done(((bf16[32,6,128,128]{3,2,1,0:T(8,128)(2,1)}), bf16[32,6,128,128]{3,2,1,0:T(8,128)(2,1)}, u32[]{:S(2)}, u32[]{:S(2)}) %all-to-all-start.1) | async-done | bytes 6291488 | tf_op jit(solution)/shard_map/all_to_all | solution.py:53
  110.3 6.2 pad_maximum_fusion
  116.5 14.3 %gather_fusion.1 = bf16[384,128,128]{2,1,0:T(8,128)(2,1)} fusion(bf16[216,128,128]{2,1,0:T(8,128)(2,1)} %pad_maximum_fusion, s32[1024]{0:T(1024)S(1)} %pad_clamp_fusion), kind=kCustom, calls=%fused_computation.1 | custom fusion | bytes 25167360 | tf_op jit(solution)/shard_map/gather | solution.py:55
  130.8 11.6 %bitcast_convert_fusion.3 = bf16[24,128,128]{1,2,0:T(8,128)(2,1)S(1)} fusion(bf16[24,16,128,128]{3,2,1,0:T(8,128)(2,1)} %param.6, bf16[24,16,128,128]{3,2,1,0:T(8,128)(2,1)} %bitcast.96), kind=kOutput, calls=%fused_computation.16 | convolution fusion | flops 1611005952 | bytes 25952256 | tf_op jit(solution)/shard_map/rkab,rkbc->rac/dot_general | solution.py:56
  142.4 0.3 copy.45
  142.7 14.6 %all_to_all.94 = bf16[4,768,128]{1,2,0:T(8,128)(2,1)S(1)} all-to-all(bf16[4,768,128]{1,2,0:T(8,128)(2,1)S(1)} %copy.45), channel_id=1, replica_groups=mesh['mesh'=32,'state'=4] {'state'}, dimensions={0} | all-to-all | bytes 1572864 | tf_op jit(solution)/shard_map/all_to_all | solution.py:64
  157.3 2.5 convolution_convert_fusion.1
  159.8 0.4 copy.46
  160.2 12.1 %all_to_all.95 = bf16[768,4,128]{2,0,1:T(8,128)(2,1)S(1)} all-to-all(bf16[768,4,128]{2,0,1:T(8,128)(2,1)S(1)} %copy.46), channel_id=1, replica_groups=mesh['mesh'=32,'state'=4] {'state'}, dimensions={1} | all-to-all | bytes 1572864 | tf_op jit(solution)/shard_map/all_to_all | solution.py:72
  172.2 16.3 %fusion.6 = f32[24,128,16,128]{3,1,2,0:T(8,128)} fusion(bf16[24,128,128,1]{2,1,3,0:T(8,128)(2,1)S(1)} %bitcast.97, bf16[24,16,128,128]{3,2,1,0:T(8,128)(2,1)} %param.6), kind=kOutput, calls=%fused_computation.46 | convolution fusion | flops 1610612736 | bytes 38535168 | tf_op jit(solution)/shard_map/rkab,rac->rkbc/dot_general | solution.py:74
  188.5 24.7 %copy.48 = f32[384,128,128]{2,1,0:T(8,128)} copy(f32[384,128,128]{1,2,0:T(8,128)} %bitcast.84) | data formatting | bytes 50331648 | tf_op jit(solution)/shard_map/reshape | solution.py:78
  213.2 6.8 broadcast.272.clone
  220.0 79.3 %scatter_fusion = f32[216,128,128]{2,1,0:T(8,128)} fusion(f32[216,128,128]{2,1,0:T(8,128)} %broadcast.272.clone, s32[384]{0:T(512)S(1)} %get-tuple-element.3, f32[384,128,128]{2,1,0:T(8,128)} %copy.48), kind=kCustom, calls=%fused_computation.4 | custom fusion | flops 6291456 | bytes 75499008 | tf_op jit(solution)/shard_map/scatter-add | solution.py:77
  299.3 9.8 %convert.10 = bf16[216,128,128]{2,1,0:T(8,128)(2,1)} convert(f32[216,128,128]{2,1,0:T(8,128)} %scatter_fusion) | non-fusion elementwise | flops 3538944 | bytes 21233664 | tf_op jit(solution)/shard_map/convert.5
  309.1 8.0 slice.29
  317.1 9.1 %all-to-all-start.4 = ((bf16[32,6,128,128]{3,2,1,0:T(8,128)(2,1)}), bf16[32,6,128,128]{3,2,1,0:T(8,128)(2,1)}, u32[]{:S(2)}, u32[]{:S(2)}) async-start(bf16[32,6,128,128]{3,2,1,0:T(8,128)(2,1)} %bitcast.91), calls=%async_computation.4 | async-start | bytes 12582912 | tf_op jit(solution)/shard_map/all_to_all | solution.py:86
  326.3 0.5 broadcast.300
  326.8 0.7 reduce.6
  327.5 0.1 reshape.387
  327.6 0.2 convert_element_type.68
  327.8 76.3 %all-to-all-done.4 = bf16[32,6,128,128]{3,2,1,0:T(8,128)(2,1)} async-done(((bf16[32,6,128,128]{3,2,1,0:T(8,128)(2,1)}), bf16[32,6,128,128]{3,2,1,0:T(8,128)(2,1)}, u32[]{:S(2)}, u32[]{:S(2)}) %all-to-all-start.4) | async-done | bytes 6291488 | tf_op jit(solution)/shard_map/all_to_all | solution.py:86
  404.1 8.9 %bitcast_convert_fusion.1 = f32[192,128,128]{2,1,0:T(8,128)} fusion(bf16[32,6,128,128]{3,2,1,0:T(8,128)(2,1)} %all-to-all-done.4), kind=kLoop, calls=%fused_computation.11 | loop fusion | flops 3145728 | bytes 18874368 | tf_op jit(solution)/shard_map/convert_element_type | solution.py:87
  412.9 25.3 %scatter_fusion.1 = f32[24,128,128]{2,1,0:T(8,128)S(1)} fusion(f32[24,128,128]{2,1,0:T(8,128)S(1)} %convert_element_type.68, s32[192]{0:T(256)S(1)} %reshape.387, f32[192,128,128]{2,1,0:T(8,128)} %bitcast_convert_fusion.1), kind=kCustom, calls=%fused_computation.5 | custom fusion | flops 3145728 | bytes 37749504 | tf_op jit(solution)/shard_map/scatter-add | solution.py:88
  438.2 1.6 fusion
  439.8 7.9 gather_fusion.2
  447.8 77.9 %all_to_all.96 = bf16[32,6,128,128]{3,2,1,0:T(8,128)(2,1)S(1)} all-to-all(bf16[32,6,128,128]{3,2,1,0:T(8,128)(2,1)} %bitcast.94), channel_id=1, replica_groups=mesh['mesh'=32,'state'=4] {'mesh'}, dimensions={0} | all-to-all | bytes 12582912 | tf_op jit(solution)/shard_map/all_to_all | solution.py:53
  525.6 3.5 pad_maximum_fusion.1
  529.1 14.3 %gather_fusion.3 = bf16[384,128,128]{2,1,0:T(8,128)(2,1)} fusion(bf16[216,128,128]{2,1,0:T(8,128)(2,1)} %pad_maximum_fusion.1, s32[1024]{0:T(1024)S(1)} %pad_clamp_fusion), kind=kCustom, calls=%fused_computation.3 | custom fusion | bytes 25167360 | tf_op jit(solution)/shard_map/gather | solution.py:55
  543.4 11.6 %bitcast_convert_fusion.2 = bf16[24,128,128]{1,2,0:T(8,128)(2,1)S(1)} fusion(bf16[24,16,128,128]{3,2,1,0:T(8,128)(2,1)} %param.6, bf16[24,16,128,128]{3,2,1,0:T(8,128)(2,1)} %bitcast.95), kind=kOutput, calls=%fused_computation.13 | convolution fusion | flops 1611005952 | bytes 25952256 | tf_op jit(solution)/shard_map/rkab,rkbc->rac/dot_general | solution.py:56
  555.0 0.3 copy.49
  555.3 15.3 %all_to_all.97 = bf16[4,768,128]{1,2,0:T(8,128)(2,1)S(1)} all-to-all(bf16[4,768,128]{1,2,0:T(8,128)(2,1)S(1)} %copy.49), channel_id=1, replica_groups=mesh['mesh'=32,'state'=4] {'state'}, dimensions={0} | all-to-all | bytes 1572864 | tf_op jit(solution)/shard_map/all_to_all | solution.py:64
  570.5 2.1 convolution_divide_fusion
  572.6 0.6 convolution_convert_fusion
  573.3 0.5 copy-done.1
  573.8 0.4 copy.50
  574.1 14.7 %all_to_all.98 = bf16[768,4,128]{2,0,1:T(8,128)(2,1)S(1)} all-to-all(bf16[768,4,128]{2,0,1:T(8,128)(2,1)S(1)} %copy.50), channel_id=1, replica_groups=mesh['mesh'=32,'state'=4] {'state'}, dimensions={1} | all-to-all | bytes 1572864 | tf_op jit(solution)/shard_map/all_to_all | solution.py:72
  588.8 16.3 %fusion.7 = f32[24,128,16,128]{3,1,2,0:T(8,128)} fusion(bf16[24,128,128,1]{2,1,3,0:T(8,128)(2,1)S(1)} %bitcast.98, bf16[24,16,128,128]{3,2,1,0:T(8,128)(2,1)} %param.6), kind=kOutput, calls=%fused_computation.47 | convolution fusion | flops 1610612736 | bytes 38535168 | tf_op jit(solution)/shard_map/rkab,rac->rkbc/dot_general | solution.py:74
  605.2 24.7 %copy.52 = f32[384,128,128]{2,1,0:T(8,128)} copy(f32[384,128,128]{1,2,0:T(8,128)} %bitcast.85) | data formatting | bytes 50331648 | tf_op jit(solution)/shard_map/reshape | solution.py:78
  629.8 6.8 broadcast.272
  636.7 79.3 %scatter_fusion.2 = f32[216,128,128]{2,1,0:T(8,128)} fusion(f32[216,128,128]{2,1,0:T(8,128)} %broadcast.272, s32[384]{0:T(512)S(1)} %get-tuple-element.3, f32[384,128,128]{2,1,0:T(8,128)} %copy.52), kind=kCustom, calls=%fused_computation.6 | custom fusion | flops 6291456 | bytes 75499008 | tf_op jit(solution)/shard_map/scatter-add | solution.py:77
  716.0 9.8 %convert.11 = bf16[216,128,128]{2,1,0:T(8,128)(2,1)} convert(f32[216,128,128]{2,1,0:T(8,128)} %scatter_fusion.2) | non-fusion elementwise | flops 3538944 | bytes 21233664 | tf_op jit(solution)/shard_map/convert.3
  725.7 8.0 slice.31
  733.8 5.0 all-to-all-start.8
  738.8 0.2 convert_element_type.77
  739.0 77.7 %all-to-all-done.8 = bf16[32,6,128,128]{3,2,1,0:T(8,128)(2,1)} async-done(((bf16[32,6,128,128]{3,2,1,0:T(8,128)(2,1)}), bf16[32,6,128,128]{3,2,1,0:T(8,128)(2,1)}, u32[]{:S(2)}, u32[]{:S(2)}) %all-to-all-start.8) | async-done | bytes 6291488 | tf_op jit(solution)/shard_map/all_to_all | solution.py:86
  816.7 8.9 %bitcast_convert_fusion = f32[192,128,128]{2,1,0:T(8,128)} fusion(bf16[32,6,128,128]{3,2,1,0:T(8,128)(2,1)} %all-to-all-done.8), kind=kLoop, calls=%fused_computation.10 | loop fusion | flops 3145728 | bytes 18874368 | tf_op jit(solution)/shard_map/convert_element_type | solution.py:87
  825.6 25.3 %scatter_fusion.3 = f32[24,128,128]{2,1,0:T(8,128)S(1)} fusion(f32[24,128,128]{2,1,0:T(8,128)S(1)} %convert_element_type.77, s32[192]{0:T(256)S(1)} %reshape.387, f32[192,128,128]{2,1,0:T(8,128)} %bitcast_convert_fusion), kind=kCustom, calls=%fused_computation.7 | custom fusion | flops 3145728 | bytes 37749504 | tf_op jit(solution)/shard_map/scatter-add | solution.py:88
  850.9 2.8 bitcast_divide_fusion
  (24 shorter events, 0.7 us)
Async XLA Ops:
  0.6 156.7 %copy-start = (bf16[512,512]{1,0:T(8,128)(2,1)S(1)}, bf16[512,512]{1,0:T(8,128)(2,1)}, u32[]{:S(2)}) copy-start(bf16[512,512]{1,0:T(8,128)(2,1)} %param.8) | copy-start | bytes 1572868
  4.4 14.7 %all-to-all-start = ((s32[32,1,6]{2,1,0:T(1,128)}), s32[32,1,6]{2,1,0:T(1,128)S(1)}, u32[]{:S(2)}, u32[]{:S(2)}) async-start(s32[32,1,6]{2,1,0:T(1,128)} %copy.44), calls=%async_computation | async-start | bytes 32768 | tf_op jit(solution)/shard_map/all_to_all | solution.py:45
  27.1 83.2 %all-to-all-start.1 = ((bf16[32,6,128,128]{3,2,1,0:T(8,128)(2,1)}), bf16[32,6,128,128]{3,2,1,0:T(8,128)(2,1)}, u32[]{:S(2)}, u32[]{:S(2)}) async-start(bf16[32,6,128,128]{3,2,1,0:T(8,128)(2,1)} %bitcast.90), calls=%async_computation.1 | async-start | bytes 12582912 | tf_op jit(solution)/shard_map/all_to_all | solution.py:53
  317.1 10.4 %slice-start = ((bf16[216,128,128]{2,1,0:T(8,128)(2,1)}), bf16[24,128,128]{2,1,0:T(8,128)(2,1)S(1)}, s32[]{:S(2)}) async-start(bf16[216,128,128]{2,1,0:T(8,128)(2,1)} %convert.10), calls=%async_computation.9 | async-start | bytes 1572864 | tf_op jit(solution)/shard_map/slice | solution.py:80
  317.1 86.9 %all-to-all-start.4 = ((bf16[32,6,128,128]{3,2,1,0:T(8,128)(2,1)}), bf16[32,6,128,128]{3,2,1,0:T(8,128)(2,1)}, u32[]{:S(2)}, u32[]{:S(2)}) async-start(bf16[32,6,128,128]{3,2,1,0:T(8,128)(2,1)} %bitcast.91), calls=%async_computation.4 | async-start | bytes 12582912 | tf_op jit(solution)/shard_map/all_to_all | solution.py:86
  572.6 1.1 copy-start.1
  733.8 5.1 slice-start.1
  733.8 83.0 %all-to-all-start.8 = ((bf16[32,6,128,128]{3,2,1,0:T(8,128)(2,1)}), bf16[32,6,128,128]{3,2,1,0:T(8,128)(2,1)}, u32[]{:S(2)}, u32[]{:S(2)}) async-start(bf16[32,6,128,128]{3,2,1,0:T(8,128)(2,1)} %bitcast.92), calls=%async_computation.8 | async-start | bytes 12582912 | tf_op jit(solution)/shard_map/all_to_all | solution.py:86
where the time goes:
time: 862 us; the launch traced here: 854 us
  other arithmetic  266 us (31%)
  waiting for transfers between devices  237 us (27%)
  blocking collectives  134 us (16%)
  local copies, waits for them, and re-layouts  128 us (15%)
  matrix products  61 us (7%)
  starting transfers between devices  27 us (3%)
    scatter-add x2, other arithmetic, per_device(): jax.ops.segment_sum(spread.reshape(-1, block_size, state_cols), sources,...  159 us
    all_to_all x2, waiting for transfers between devices, per_device(): lax.all_to_all(outgoing, 'mesh', split_axis=0, concat_axis=0, tiled=True)  154 us
    all_to_all x1, blocking collectives, per_device(): lax.all_to_all(blocks[asked], 'mesh', split_axis=0, concat_axis=0, tiled=...  77.9 us
    all_to_all x1, waiting for transfers between devices, per_device(): lax.all_to_all(blocks[asked], 'mesh', split_axis=0, concat_axis=0, tiled=...  77.2 us
    scatter-add x2, other arithmetic, per_device(): jax.ops.segment_sum(arriving, flat_asked, num_segments=block_rows)  50.5 us
    reshape x2, local copies, waits for them, and re-layouts, per_device(): spread.reshape(-1, block_size, state_cols)  49.3 us
    dot_general x2, matrix products, per_device(): jnp.einsum('rkab,rac->rkbc', kern_blocks, returned, preferred_element_typ...  32.7 us
    all_to_all x2, blocking collectives, per_device(): lax.all_to_all(pieces, 'state', split_axis=0, concat_axis=2, tiled=True)  29.9 us
  transfers between devices with their start and end apart: 4, of which 4 were waited for; matrix products, arithmetic and copies ran while one was open for 0% of the time, Pallas kernels for 0%

commit v1 on v0

--- a/solution.py
+++ b/solution.py
@@ -61,7 +61,12 @@
         )
         mixed = jnp.einsum(
             "xrl,jl->xrj",
-            lax.all_to_all(pieces, "state", split_axis=0, concat_axis=2, tiled=True),
+            jnp.concatenate(
+                lax.all_to_all(
+                    jnp.stack(jnp.split(pieces, lax.axis_size("state"), axis=0)), "state", 0, 0
+                ),
+                axis=2,
+            ),
             state_kernel,
             preferred_element_type=jnp.float32,
         )

time: 862 us -> 863 us (level)
    another operation x2 -> x4, other arithmetic: 19.5 us -> 19.7 us
where the time goes in v1:
time: 863 us; the launch traced here: 855 us
  other arithmetic  266 us (31%)
  waiting for transfers between devices  237 us (27%)
  blocking collectives  134 us (16%)
  local copies, waits for them, and re-layouts  128 us (15%)
  matrix products  61 us (7%)
  starting transfers between devices  27 us (3%)
    scatter-add x2, other arithmetic, per_device(): jax.ops.segment_sum(spread.reshape(-1, block_size, state_cols), sources,...  159 us
    all_to_all x2, waiting for transfers between devices, per_device(): lax.all_to_all(outgoing, 'mesh', split_axis=0, concat_axis=0, tiled=True)  154 us
    all_to_all x1, blocking collectives, per_device(): lax.all_to_all(blocks[asked], 'mesh', split_axis=0, concat_axis=0, tiled=...  77.9 us
    all_to_all x1, waiting for transfers between devices, per_device(): lax.all_to_all(blocks[asked], 'mesh', split_axis=0, concat_axis=0, tiled=...  77.2 us
    scatter-add x2, other arithmetic, per_device(): jax.ops.segment_sum(arriving, flat_asked, num_segments=block_rows)  50.5 us
    reshape x2, local copies, waits for them, and re-layouts, per_device(): spread.reshape(-1, block_size, state_cols)  49.3 us
    dot_general x2, matrix products, per_device(): jnp.einsum('rkab,rac->rkbc', kern_blocks, returned, preferred_element_typ...  32.7 us
    all_to_all x2, blocking collectives, per_device(): lax.all_to_all(jnp.stack(jnp.split(pieces, lax.axis_size('state'), axis=0...  29.9 us
  transfers between devices with their start and end apart: 4, of which 4 were waited for; matrix products, arithmetic and copies ran while one was open for 0% of the time, Pallas kernels for 0%

profile of v1, /device:TPU:0, one launch (start us, length us, event | category | flops | bytes accessed | tf_op | source)
XLA Modules:
  0.0 855.1 jit_solution(6568671776467171781)
XLA Ops:
  0.6 0.8 broadcast_divide_fusion
  1.4 0.7 sign_compare_fusion
  2.7 0.6 fusion.3
  3.4 0.2 reduce_window_sum.11
  3.7 0.7 copy.58
  4.4 7.4 all-to-all-start
  11.8 1.5 convert_element_type.63
  13.3 5.8 all-to-all-done
  19.2 7.9 gather_fusion
  27.1 5.4 all-to-all-start.1
  32.8 0.2 fusion.4
  33.1 77.2 %all-to-all-done.1 = bf16[32,6,128,128]{3,2,1,0:T(8,128)(2,1)} async-done(((bf16[32,6,128,128]{3,2,1,0:T(8,128)(2,1)}), bf16[32,6,128,128]{3,2,1,0:T(8,128)(2,1)}, u32[]{:S(2)}, u32[]{:S(2)}) %all-to-all-start.1) | async-done | bytes 6291488 | tf_op jit(solution)/shard_map/all_to_all | solution.py:53
  110.3 6.2 pad_maximum_fusion
  116.5 14.3 %gather_fusion.1 = bf16[384,128,128]{2,1,0:T(8,128)(2,1)} fusion(bf16[216,128,128]{2,1,0:T(8,128)(2,1)} %pad_maximum_fusion, s32[1024]{0:T(1024)S(1)} %pad_clamp_fusion), kind=kCustom, calls=%fused_computation.1 | custom fusion | bytes 25167360 | tf_op jit(solution)/shard_map/gather | solution.py:55
  130.8 11.6 %fusion.1 = bf16[24,128,128]{2,1,0:T(8,128)(2,1)S(1)} fusion(bf16[24,16,128,128]{3,2,1,0:T(8,128)(2,1)} %param.6, bf16[24,16,128,128]{3,2,1,0:T(8,128)(2,1)} %bitcast.106), kind=kOutput, calls=%fused_computation.23 | convolution fusion | flops 1611005952 | bytes 25952256 | tf_op jit(solution)/shard_map/rkab,rkbc->rac/dot_general | solution.py:56
  142.5 0.1 copy.59
  142.6 0.1 copy.60
  142.8 0.1 copy.61
  142.9 0.1 copy.62
  143.2 14.6 %all_to_all.74 = bf16[4,1,768,128]{2,3,1,0:T(8,128)(2,1)S(1)} all-to-all(bf16[4,1,768,128]{2,3,1,0:T(8,128)(2,1)S(1)} %pad_maximum_fusion.2), channel_id=1, replica_groups=mesh['mesh'=32,'state'=4] {'state'}, dimensions={0} | all-to-all | bytes 1572864 | tf_op jit(solution)/shard_map/all_to_all | solution.py:65
  157.8 2.4 convolution_convert_fusion.1
  160.3 0.4 copy.64
  160.6 12.1 %all_to_all.75 = bf16[768,4,128]{2,0,1:T(8,128)(2,1)S(1)} all-to-all(bf16[768,4,128]{2,0,1:T(8,128)(2,1)S(1)} %copy.64), channel_id=1, replica_groups=mesh['mesh'=32,'state'=4] {'state'}, dimensions={1} | all-to-all | bytes 1572864 | tf_op jit(solution)/shard_map/all_to_all | solution.py:77
  172.7 16.3 %fusion.10 = f32[24,128,16,128]{3,1,2,0:T(8,128)} fusion(bf16[24,128,128,1]{2,1,3,0:T(8,128)(2,1)S(1)} %bitcast.107, bf16[24,16,128,128]{3,2,1,0:T(8,128)(2,1)} %param.6), kind=kOutput, calls=%fused_computation.52 | convolution fusion | flops 1610612736 | bytes 38535168 | tf_op jit(solution)/shard_map/rkab,rac->rkbc/dot_general | solution.py:79
  189.0 24.7 %copy.66 = f32[384,128,128]{2,1,0:T(8,128)} copy(f32[384,128,128]{1,2,0:T(8,128)} %bitcast.94) | data formatting | bytes 50331648 | tf_op jit(solution)/shard_map/reshape | solution.py:83
  213.7 6.8 broadcast.272.clone
  220.5 79.3 %scatter_fusion = f32[216,128,128]{2,1,0:T(8,128)} fusion(f32[216,128,128]{2,1,0:T(8,128)} %broadcast.272.clone, s32[384]{0:T(512)S(1)} %get-tuple-element.3, f32[384,128,128]{2,1,0:T(8,128)} %copy.66), kind=kCustom, calls=%fused_computation.4 | custom fusion | flops 6291456 | bytes 75499008 | tf_op jit(solution)/shard_map/scatter-add | solution.py:82
  299.8 9.8 %convert.10 = bf16[216,128,128]{2,1,0:T(8,128)(2,1)} convert(f32[216,128,128]{2,1,0:T(8,128)} %scatter_fusion) | non-fusion elementwise | flops 3538944 | bytes 21233664 | tf_op jit(solution)/shard_map/convert.5
  309.6 8.0 slice.37
  317.6 9.1 %all-to-all-start.4 = ((bf16[32,6,128,128]{3,2,1,0:T(8,128)(2,1)}), bf16[32,6,128,128]{3,2,1,0:T(8,128)(2,1)}, u32[]{:S(2)}, u32[]{:S(2)}) async-start(bf16[32,6,128,128]{3,2,1,0:T(8,128)(2,1)} %bitcast.101), calls=%async_computation.4 | async-start | bytes 12582912 | tf_op jit(solution)/shard_map/all_to_all | solution.py:91
  326.7 0.5 broadcast.300
  327.2 0.7 reduce.6
  328.1 0.2 convert_element_type.68
  328.2 76.3 %all-to-all-done.4 = bf16[32,6,128,128]{3,2,1,0:T(8,128)(2,1)} async-done(((bf16[32,6,128,128]{3,2,1,0:T(8,128)(2,1)}), bf16[32,6,128,128]{3,2,1,0:T(8,128)(2,1)}, u32[]{:S(2)}, u32[]{:S(2)}) %all-to-all-start.4) | async-done | bytes 6291488 | tf_op jit(solution)/shard_map/all_to_all | solution.py:91
  404.6 8.9 %bitcast_convert_fusion.1 = f32[192,128,128]{2,1,0:T(8,128)} fusion(bf16[32,6,128,128]{3,2,1,0:T(8,128)(2,1)} %all-to-all-done.4), kind=kLoop, calls=%fused_computation.11 | loop fusion | flops 3145728 | bytes 18874368 | tf_op jit(solution)/shard_map/convert_element_type | solution.py:92
  413.4 25.3 %scatter_fusion.1 = f32[24,128,128]{2,1,0:T(8,128)S(1)} fusion(f32[24,128,128]{2,1,0:T(8,128)S(1)} %convert_element_type.68, s32[192]{0:T(256)S(1)} %reshape.407, f32[192,128,128]{2,1,0:T(8,128)} %bitcast_convert_fusion.1), kind=kCustom, calls=%fused_computation.5 | custom fusion | flops 3145728 | bytes 37749504 | tf_op jit(solution)/shard_map/scatter-add | solution.py:93
  438.7 1.6 fusion
  440.3 7.9 gather_fusion.2
  448.2 77.9 %all_to_all.76 = bf16[32,6,128,128]{3,2,1,0:T(8,128)(2,1)S(1)} all-to-all(bf16[32,6,128,128]{3,2,1,0:T(8,128)(2,1)} %bitcast.104), channel_id=1, replica_groups=mesh['mesh'=32,'state'=4] {'mesh'}, dimensions={0} | all-to-all | bytes 12582912 | tf_op jit(solution)/shard_map/all_to_all | solution.py:53
  526.1 3.5 pad_maximum_fusion.1
  529.6 14.3 %gather_fusion.3 = bf16[384,128,128]{2,1,0:T(8,128)(2,1)} fusion(bf16[216,128,128]{2,1,0:T(8,128)(2,1)} %pad_maximum_fusion.1, s32[1024]{0:T(1024)S(1)} %pad_clamp_fusion), kind=kCustom, calls=%fused_computation.3 | custom fusion | bytes 25167360 | tf_op jit(solution)/shard_map/gather | solution.py:55
  543.9 11.6 %fusion.2 = bf16[24,128,128]{2,1,0:T(8,128)(2,1)S(1)} fusion(bf16[24,16,128,128]{3,2,1,0:T(8,128)(2,1)} %param.6, bf16[24,16,128,128]{3,2,1,0:T(8,128)(2,1)} %bitcast.105), kind=kOutput, calls=%fused_computation.24 | convolution fusion | flops 1611005952 | bytes 25952256 | tf_op jit(solution)/shard_map/rkab,rkbc->rac/dot_general | solution.py:56
  555.5 0.1 copy.67
  555.7 0.1 copy.68
  555.8 0.1 copy.69
  556.0 0.1 copy.70
  556.3 15.3 %all_to_all.77 = bf16[4,1,768,128]{2,3,1,0:T(8,128)(2,1)S(1)} all-to-all(bf16[4,1,768,128]{2,3,1,0:T(8,128)(2,1)S(1)} %pad_maximum_fusion.3), channel_id=1, replica_groups=mesh['mesh'=32,'state'=4] {'state'}, dimensions={0} | all-to-all | bytes 1572864 | tf_op jit(solution)/shard_map/all_to_all | solution.py:65
  571.5 2.1 convolution_divide_fusion
  573.6 0.6 convolution_convert_fusion
  574.2 0.5 copy-done.1
  574.7 0.4 copy.72
  575.1 14.7 %all_to_all.78 = bf16[768,4,128]{2,0,1:T(8,128)(2,1)S(1)} all-to-all(bf16[768,4,128]{2,0,1:T(8,128)(2,1)S(1)} %copy.72), channel_id=1, replica_groups=mesh['mesh'=32,'state'=4] {'state'}, dimensions={1} | all-to-all | bytes 1572864 | tf_op jit(solution)/shard_map/all_to_all | solution.py:77
  589.8 16.3 %fusion.11 = f32[24,128,16,128]{3,1,2,0:T(8,128)} fusion(bf16[24,128,128,1]{2,1,3,0:T(8,128)(2,1)S(1)} %bitcast.108, bf16[24,16,128,128]{3,2,1,0:T(8,128)(2,1)} %param.6), kind=kOutput, calls=%fused_computation.53 | convolution fusion | flops 1610612736 | bytes 38535168 | tf_op jit(solution)/shard_map/rkab,rac->rkbc/dot_general | solution.py:79
  606.1 24.7 %copy.74 = f32[384,128,128]{2,1,0:T(8,128)} copy(f32[384,128,128]{1,2,0:T(8,128)} %bitcast.95) | data formatting | bytes 50331648 | tf_op jit(solution)/shard_map/reshape | solution.py:83
  630.8 6.8 broadcast.272
  637.6 79.3 %scatter_fusion.2 = f32[216,128,128]{2,1,0:T(8,128)} fusion(f32[216,128,128]{2,1,0:T(8,128)} %broadcast.272, s32[384]{0:T(512)S(1)} %get-tuple-element.3, f32[384,128,128]{2,1,0:T(8,128)} %copy.74), kind=kCustom, calls=%fused_computation.6 | custom fusion | flops 6291456 | bytes 75499008 | tf_op jit(solution)/shard_map/scatter-add | solution.py:82
  716.9 9.8 %convert.11 = bf16[216,128,128]{2,1,0:T(8,128)(2,1)} convert(f32[216,128,128]{2,1,0:T(8,128)} %scatter_fusion.2) | non-fusion elementwise | flops 3538944 | bytes 21233664 | tf_op jit(solution)/shard_map/convert.3
  726.7 8.0 slice.39
  734.7 5.0 all-to-all-start.8
  739.8 0.2 convert_element_type.77
  740.0 77.7 %all-to-all-done.8 = bf16[32,6,128,128]{3,2,1,0:T(8,128)(2,1)} async-done(((bf16[32,6,128,128]{3,2,1,0:T(8,128)(2,1)}), bf16[32,6,128,128]{3,2,1,0:T(8,128)(2,1)}, u32[]{:S(2)}, u32[]{:S(2)}) %all-to-all-start.8) | async-done | bytes 6291488 | tf_op jit(solution)/shard_map/all_to_all | solution.py:91
  817.7 8.9 %bitcast_convert_fusion = f32[192,128,128]{2,1,0:T(8,128)} fusion(bf16[32,6,128,128]{3,2,1,0:T(8,128)(2,1)} %all-to-all-done.8), kind=kLoop, calls=%fused_computation.10 | loop fusion | flops 3145728 | bytes 18874368 | tf_op jit(solution)/shard_map/convert_element_type | solution.py:92
  826.6 25.3 %scatter_fusion.3 = f32[24,128,128]{2,1,0:T(8,128)S(1)} fusion(f32[24,128,128]{2,1,0:T(8,128)S(1)} %convert_element_type.77, s32[192]{0:T(256)S(1)} %reshape.407, f32[192,128,128]{2,1,0:T(8,128)} %bitcast_convert_fusion), kind=kCustom, calls=%fused_computation.7 | custom fusion | flops 3145728 | bytes 37749504 | tf_op jit(solution)/shard_map/scatter-add | solution.py:93
  851.8 2.8 bitcast_divide_fusion
  (34 shorter events, 1.5 us)
Async XLA Ops:
  0.6 157.2 %copy-start = (bf16[512,512]{1,0:T(8,128)(2,1)S(1)}, bf16[512,512]{1,0:T(8,128)(2,1)}, u32[]{:S(2)}) copy-start(bf16[512,512]{1,0:T(8,128)(2,1)} %param.8) | copy-start | bytes 1572868
  4.4 14.7 %all-to-all-start = ((s32[32,1,6]{2,1,0:T(1,128)}), s32[32,1,6]{2,1,0:T(1,128)S(1)}, u32[]{:S(2)}, u32[]{:S(2)}) async-start(s32[32,1,6]{2,1,0:T(1,128)} %copy.58), calls=%async_computation | async-start | bytes 32768 | tf_op jit(solution)/shard_map/all_to_all | solution.py:45
  27.1 83.2 %all-to-all-start.1 = ((bf16[32,6,128,128]{3,2,1,0:T(8,128)(2,1)}), bf16[32,6,128,128]{3,2,1,0:T(8,128)(2,1)}, u32[]{:S(2)}, u32[]{:S(2)}) async-start(bf16[32,6,128,128]{3,2,1,0:T(8,128)(2,1)} %bitcast.100), calls=%async_computation.1 | async-start | bytes 12582912 | tf_op jit(solution)/shard_map/all_to_all | solution.py:53
  317.6 10.4 %slice-start = ((bf16[216,128,128]{2,1,0:T(8,128)(2,1)}), bf16[24,128,128]{2,1,0:T(8,128)(2,1)S(1)}, s32[]{:S(2)}) async-start(bf16[216,128,128]{2,1,0:T(8,128)(2,1)} %convert.10), calls=%async_computation.9 | async-start | bytes 1572864 | tf_op jit(solution)/shard_map/slice | solution.py:85
  317.6 86.9 %all-to-all-start.4 = ((bf16[32,6,128,128]{3,2,1,0:T(8,128)(2,1)}), bf16[32,6,128,128]{3,2,1,0:T(8,128)(2,1)}, u32[]{:S(2)}, u32[]{:S(2)}) async-start(bf16[32,6,128,128]{3,2,1,0:T(8,128)(2,1)} %bitcast.101), calls=%async_computation.4 | async-start | bytes 12582912 | tf_op jit(solution)/shard_map/all_to_all | solution.py:91
  573.6 1.1 copy-start.1
  734.7 5.1 slice-start.1
  734.7 83.0 %all-to-all-start.8 = ((bf16[32,6,128,128]{3,2,1,0:T(8,128)(2,1)}), bf16[32,6,128,128]{3,2,1,0:T(8,128)(2,1)}, u32[]{:S(2)}, u32[]{:S(2)}) async-start(bf16[32,6,128,128]{3,2,1,0:T(8,128)(2,1)} %bitcast.102), calls=%async_computation.8 | async-start | bytes 12582912 | tf_op jit(solution)/shard_map/all_to_all | solution.py:91
